TPU v7x, 256 devices: a whole 4x4x8 slice. The times are simulated.
256 devices in a mesh: head: 32 (over x, z_lo, core), ctx: 8 (over y, z_hi).
Axes of the slice: x: 4, y: 4, z: 8 (z_hi: 2, z_lo: 4; z = z_hi * 4 + z_lo), core: 2. Of those that a mesh axis runs over, the one named last changes fastest.
Arguments:
- queries: bfloat16 [32768, 8192], P('ctx', 'head'), may hold values from -6 to 6
- keys: bfloat16 [1024, 512], P(('head', 'ctx')), may hold values from -6 to 6
- values: bfloat16 [1024, 512], P(('head', 'ctx')), may hold values from -6 to 6
- outputs: bfloat16 [32768, 8192], P('ctx', 'head'), may hold values from -6 to 6
- dout: bfloat16 [32768, 8192], P(('ctx', 'head')), may hold values from -24 to 24
- lse: float32 [64, 32768], P('head', 'ctx'), may hold values from 6.5 to 8.5
Outputs:
- dq: bfloat16 [32768, 8192], P('ctx', 'head')
- dk: bfloat16 [1024, 512], P(('head', 'ctx'))
- dv: bfloat16 [1024, 512], P(('head', 'ctx'))
All inputs are finite; a program needn't handle non-finite values.
Results may differ from a plain program's by a relative error of at most 0.0052.
Values may be sent and summed in bfloat16 or wider, within the bound.
A program may use at most 128 MiB of HBM per device.

v0:
```python
import jax
import jax.numpy as jnp
from jax import lax
from jax.sharding import PartitionSpec as P

QUERY_HEADS = 64
KEY_VALUE_HEADS = 4
HEAD_SIZE = 128


def on_device(queries, keys, values, outputs, dout, lse):
    factor = HEAD_SIZE ** (-0.5)
    query_head_index = lax.axis_index("head")
    present_heads = queries.shape[1] // HEAD_SIZE
    key_value_group = query_head_index * present_heads // (QUERY_HEADS // KEY_VALUE_HEADS)
    dout_local = lax.all_to_all(dout, "head", split_axis=1, concat_axis=0, tiled=True)
    full_keys, full_values = (
        lax.all_gather(keys, ("head", "ctx"), axis=0, tiled=True),
        lax.all_gather(values, ("head", "ctx"), axis=0, tiled=True),
    )
    key_group = lax.dynamic_slice_in_dim(full_keys, key_value_group * HEAD_SIZE, HEAD_SIZE, 1)
    value_group = lax.dynamic_slice_in_dim(full_values, key_value_group * HEAD_SIZE, HEAD_SIZE, 1)
    key_total_count = key_group.shape[0]
    query_count = queries.shape[0]
    block_rows = min(query_count, 512)
    dk_sum = jnp.zeros((key_total_count, HEAD_SIZE), jnp.float32)
    dv_sum = jnp.zeros((key_total_count, HEAD_SIZE), jnp.float32)
    dq_heads = []
    for local_head in range(present_heads):
        lower = local_head * HEAD_SIZE
        pieces = []
        for start in range(0, query_count, block_rows):
            q_head = queries[start : start + block_rows, lower : lower + HEAD_SIZE]
            o_head = outputs[start : start + block_rows, lower : lower + HEAD_SIZE]
            d_head = dout_local[start : start + block_rows, lower : lower + HEAD_SIZE]
            l_head = lse[local_head, start : start + block_rows]
            scores = jnp.dot(q_head, key_group.T, preferred_element_type=jnp.float32) * factor
            probs = jnp.exp(scores - l_head[:, None])
            probs_low = probs.astype(jnp.bfloat16)
            dv_sum = dv_sum + jnp.dot(probs_low.T, d_head, preferred_element_type=jnp.float32)
            dprobs = jnp.dot(d_head, value_group.T, preferred_element_type=jnp.float32)
            delta = jnp.sum(d_head.astype(jnp.float32) * o_head.astype(jnp.float32), axis=1)
            dscores = (probs * (dprobs - delta[:, None])).astype(jnp.bfloat16)
            pieces.append(
                (jnp.dot(dscores, key_group, preferred_element_type=jnp.float32) * factor).astype(
                    jnp.bfloat16
                )
            )
            dk_sum = dk_sum + jnp.dot(dscores.T, q_head, preferred_element_type=jnp.float32)
        dq_heads.append(jnp.concatenate(pieces, axis=0))
    dq_local = jnp.concatenate(dq_heads, axis=1)
    empty_buffer = jnp.zeros((key_total_count, KEY_VALUE_HEADS * HEAD_SIZE), jnp.float32)
    padded_k = lax.dynamic_update_slice_in_dim(empty_buffer, dk_sum, key_value_group * HEAD_SIZE, 1)
    padded_v = lax.dynamic_update_slice_in_dim(empty_buffer, dv_sum, key_value_group * HEAD_SIZE, 1)
    dk_local, dv_local = (
        lax.psum_scatter(padded_k, ("head", "ctx"), scatter_dimension=0, tiled=True),
        lax.psum_scatter(padded_v, ("head", "ctx"), scatter_dimension=0, tiled=True),
    )
    return (dq_local, (dk_local * factor).astype(jnp.bfloat16), dv_local.astype(jnp.bfloat16))


def solution(mesh):
    placed = (
        P("ctx", "head"),
        P(("head", "ctx"), None),
        P(("head", "ctx"), None),
        P("ctx", "head"),
        P(("ctx", "head"), None),
        P("head", "ctx"),
    )
    return jax.shard_map(
        on_device,
        mesh=mesh,
        in_specs=placed,
        out_specs=(P("ctx", "head"), P(("head", "ctx"), None), P(("head", "ctx"), None)),
        check_vma=False,
    )
```

profile of v0, /device:TPU:32, one launch (start us, length us, event | category | flops | bytes accessed | tf_op | source)
XLA Modules:
  0.0 1422.1 jit_solution(7962984657500991076)
XLA Ops:
  8.6 3.2 copy.10
  11.9 2.9 copy.11
  14.8 8.8 all-to-all-start
  23.7 523.2 %all-gather.5.cloned.1.call-done = bf16[256,4,512]{2,1,0:T(4,128)(2,1)} async-done(((bf16[1,4,512]{2,1,0:T(4,128)(2,1)}), bf16[256,4,512]{2,1,0:T(4,128)(2,1)}) %all-gather.5.cloned.1.call-update) | async-done | bytes 1048592 | tf_op jit(solution)/shard_map/all_gather | solution.py:18
  548.3 2.8 fusion.142
  551.1 2.7 fusion.139
  553.8 520.8 %all-gather.7.cloned.1.call-done = bf16[256,4,512]{2,1,0:T(4,128)(2,1)} async-done(((bf16[1,4,512]{2,1,0:T(4,128)(2,1)}), bf16[256,4,512]{2,1,0:T(4,128)(2,1)}) %all-gather.7.cloned.1.call-update) | async-done | bytes 1048592 | tf_op jit(solution)/shard_map/all_gather | solution.py:19
  1076.2 2.9 fusion.136
  1079.1 2.7 fusion.133
  1081.7 1.8 fusion.130
  1085.3 1.8 fusion.124
  1087.1 1.8 fusion.121
  1088.8 1.8 fusion.118
  1090.7 1.7 fusion.115
  1092.4 1.8 fusion.112
  1094.2 1.8 fusion.109
  1096.0 1.8 fusion.106
  1099.5 1.8 fusion.100
  1101.3 1.8 fusion.146
  1103.0 1.9 multiply_reduce_fusion.11
  1105.0 2.0 multiply_reduce_fusion.8
  1162.0 83.0 %all-reduce.6 = bf16[1024,512]{1,0:T(8,128)(2,1)} all-reduce(f32[1024,512]{1,0:T(8,128)} %fusion.16), channel_id=3, replica_groups=mesh['head'=32,'ctx'=8] {'head','ctx'}, use_global_device_ids=true, to_apply=%region_17.18.clone | all-reduce | flops 524288 | bytes 3145728
  1248.7 2.8 pad_maximum_fusion
  1251.4 162.6 %all-reduce.5.cloned.1.call-done = f32[1024,512]{1,0:T(8,128)} async-done(((f32[1024,512]{1,0:T(8,128)}), f32[1024,512]{1,0:T(8,128)}) %all-reduce.5.cloned.1.call-update) | async-done | bytes 2097168
  (144 shorter events, 67.3 us)
Async XLA Ops:
  7.2 539.7 %all-gather.5.cloned.1.call-start = ((), (), s32[]{:S(2)}) async-start(), calls=%async_computation.1 | async-start | bytes 1052672 | tf_op jit(solution)/shard_map/all_gather | solution.py:18
  7.9 1066.7 %all-gather.7.cloned.1.call-start = ((), (), s32[]{:S(2)}) async-start(), calls=%async_computation.2 | async-start | bytes 1052672 | tf_op jit(solution)/shard_map/all_gather | solution.py:19
  14.8 8.8 copy-start.31
  14.8 1088.2 %all-to-all-start = ((bf16[128,32,256]{2,0,1:T(8,128)(2,1)}), bf16[128,32,256]{2,0,1:T(8,128)(2,1)S(1)}, u32[]{:S(2)}, u32[]{:S(2)}) async-start(bf16[128,32,256]{2,0,1:T(8,128)(2,1)} %copy.11), calls=%async_computation | async-start | bytes 4194304 | tf_op jit(solution)/shard_map/all_to_all | solution.py:16
  23.6 1390.5 %all-reduce.5.cloned.1.call-start = ((), (), s32[]{:S(2)}) async-start(), calls=%async_computation.3 | async-start | bytes 4194304
  548.2 5.5 copy-start
  1076.1 2.9 copy-start.1
  1076.1 5.6 copy-start.21
  1103.0 4.0 copy-start.20
  1107.5 1.6 copy-start.22
  1107.5 2.0 copy-start.2
  1109.1 1.7 copy-start.19
  1113.3 1.6 copy-start.18
  1122.1 1.6 copy-start.13
  1124.2 1.6 copy-start.12
  1140.2 13.0 copy-start.25
  1152.7 2.0 copy-start.4
  1155.2 1.7 copy-start.23
  1158.2 1.6 copy-start.27
  1158.2 2.5 copy-start.5
  1162.0 84.4 %copy-start.3 = (bf16[1024,512]{1,0:T(8,128)(2,1)S(1)}, bf16[1024,512]{1,0:T(8,128)(2,1)}, u32[]{:S(2)}) copy-start(bf16[1024,512]{1,0:T(8,128)(2,1)} %copy-done) | copy-start | bytes 3145732
  1162.0 84.4 %copy-start.26 = (bf16[1024,512]{1,0:T(8,128)(2,1)S(1)}, bf16[1024,512]{1,0:T(8,128)(2,1)}, u32[]{:S(2)}) copy-start(bf16[1024,512]{1,0:T(8,128)(2,1)} %copy-done.25) | copy-start | bytes 3145732
  1162.0 85.5 %copy-start.24 = (bf16[1024,512]{1,0:T(8,128)(2,1)S(1)}, bf16[1024,512]{1,0:T(8,128)(2,1)}, u32[]{:S(2)}) copy-start(bf16[1024,512]{1,0:T(8,128)(2,1)} %copy-done.23) | copy-start | bytes 3145732
  1245.0 3.7 copy-start.29
  (12 other events, 18.3 us)
Sparse Core Ops, SparseCore 0:
  9.8 537.0 all-gather.4
  548.7 525.8 all-gather.6
  1158.3 255.6 all-reduce.4
where the time goes:
time: 1430 us; the launch traced here: 1420 us
  waiting for transfers between devices  1210 us (85%)
  blocking collectives  83 us (6%)
  matrix products  68.8 us (5%)
  local copies, waits for them, and re-layouts  30.8 us (2%)
  between operations  14.6 us (1%)
    all_gather x1, waiting for transfers between devices, on_device(): lax.all_gather(keys, ('head', 'ctx'), axis=0, tiled=True)  523 us
    all_gather x1, waiting for transfers between devices, on_device(): lax.all_gather(values, ('head', 'ctx'), axis=0, tiled=True)  521 us
    unnamed x4, waiting for transfers between devices  164 us
    unnamed x1, blocking collectives  83 us
    dot_general x16, matrix products, on_device(): jnp.dot(q_head, key_group.T, preferred_element_type=jnp.float32) * factor  32.4 us
  transfers between devices with their start and end apart: 4, of which 3 were waited for; matrix products, arithmetic and copies ran while one was open for 4% of the time, Pallas kernels for 0%

commit v1 on v0

v1 whole, which is shorter than its diff:
```python
import functools
import math

import jax
import jax.numpy as jnp
from jax import lax
from jax.experimental import pallas as pl
from jax.experimental.pallas import tpu as pltpu
from jax.sharding import PartitionSpec as P

MESH = pl.DeviceIdType.MESH
D = 128
T = 128
NX, NZL, NC, NY, NZH = 4, 4, 2, 4, 2
NZ = NZL * NZH
NH = NX * NZL * NC
KEYS = 1024
GROUP = 16
KB = 256
C = D ** (-0.5)
LOG2E = math.log2(math.e)
NT = (((1,), (1,)), ((), ()))
F32, BF16 = jnp.float32, jnp.bfloat16


def div(a, n):
    return lax.div(a, jnp.int32(n))


def rem(a, n):
    return lax.rem(a, jnp.int32(n))


def kernel(
    q_hbm, k_ref, v_ref, o_hbm, d_hbm, lse_ref,
    dq_hbm, dk_ref, dv_ref,
    q_vm, o_vm, d_vm, dq_vm,
    a_out, a_in, kv16, kv, kk, vv, kt,
    acc, rd_in, rc_out, rc_in, tot, rb_out, rb_in, last, ra_out, ra_in,
    d_send, d_recv, q_sem, o_sem, dq_sem,
    ka_send, ka_recv, kb_send, kb_recv, kc_send, kc_recv, kd_send, kd_recv,
    rd_send, rd_recv, rc_send, rc_recv, rb_send, rb_recv, ra_send, ra_recv,
):
    head, ctx = lax.axis_index("head"), lax.axis_index("ctx")
    x, zl, core = div(head, NZL * NC), rem(div(head, NC), NZL), rem(head, NC)
    y, zh = div(ctx, NZH), rem(ctx, NZH)
    z = zh * NZL + zl
    za, zb = div(zl, 2), rem(zl, 2)

    def device(x_=x, zl_=zl, core_=core, y_=y, zh_=zh):
        return ((x_ * NZL + zl_) * NC + core_, y_ * NZH + zh_)

    def partner(j, way):
        da, dc, db, dx = rem(j, 2), rem(div(j, 2), 2), rem(div(j, 4), 2), div(j, 8)
        x_ = rem(x + NX + way * dx, NX)
        zl_ = rem(za + da, 2) * 2 + rem(zb + db, 2)
        return (x_ * NZL + zl_) * NC + rem(core + dc, NC)

    q_copy = pltpu.make_async_copy(q_hbm, q_vm, q_sem)
    o_copy = pltpu.make_async_copy(o_hbm, o_vm, o_sem)
    own = pltpu.make_async_copy(
        d_hbm.at[:, pl.ds(pl.multiple_of(head * 2 * D, 2 * D), 2 * D)], d_vm.at[head], d_recv.at[0]
    )

    barrier = pltpu.get_barrier_semaphore()

    @pl.loop(1, NH)
    def _(j):
        pl.semaphore_signal(barrier, inc=1, device_id=(partner(j, 1), ctx), device_id_type=MESH)

    for r in range(1, NY):
        pl.semaphore_signal(barrier, inc=1, device_id=device(y_=rem(y + r, NY)), device_id_type=MESH)
    for r in range(NZL):
        pl.semaphore_signal(
            barrier, inc=1, device_id=device(zl_=rem(zl + r, NZL), zh_=1 - zh), device_id_type=MESH
        )
    own.start()
    q_copy.start()
    o_copy.start()
    for g in range(NX):
        a_out[g, 0:4, :] = k_ref[:, g * D : (g + 1) * D].astype(F32)
        a_out[g, 4:8, :] = v_ref[:, g * D : (g + 1) * D].astype(F32)
    pl.semaphore_wait(barrier, NH - 1 + NY - 1 + NZL)

    def exchange(n, me, target, src, dst, send, recv):
        copies = []
        for r in range(1, n):
            to = rem(me + r, n)
            copy = pltpu.make_async_remote_copy(
                src_ref=src(to), dst_ref=dst(me), send_sem=send.at[r], recv_sem=recv.at[r],
                device_id=target(to), device_id_type=MESH,
            )
            copy.start()
            copies.append(copy)
        return copies

    ka = exchange(NX, x, lambda i: device(x_=i), lambda i: a_out.at[i], lambda i: a_in.at[i], ka_send, ka_recv)

    def block_copy(j):
        to = partner(j, 1)
        return pltpu.make_async_remote_copy(
            src_ref=d_hbm.at[:, pl.ds(pl.multiple_of(to * 2 * D, 2 * D), 2 * D)],
            dst_ref=d_vm.at[head],
            send_sem=d_send.at[j], recv_sem=d_recv.at[j],
            device_id=(to, ctx), device_id_type=MESH,
        )

    @pl.loop(1, NH)
    def _(j):
        block_copy(j).start()

    a_in[x] = a_out[x]
    for copy in ka:
        copy.wait()
    for p in range(NX):
        kv16[0, 4 * p : 4 * p + 4, :] = a_in[p, 0:4, :]
        kv16[1, 4 * p : 4 * p + 4, :] = a_in[p, 4:8, :]
    kv[core, y, z] = kv16[...].astype(BF16)

    def zdev(i):
        return device(zl_=rem(i, NZL), zh_=div(i, NZL))

    kb = exchange(NZ, z, zdev, lambda i: kv.at[core, y, z], lambda i: kv.at[core, y, i], kb_send, kb_recv)
    acc[...] = jnp.zeros_like(acc)
    for copy in kb:
        copy.wait()
    kc = exchange(NY, y, lambda i: device(y_=i), lambda i: kv.at[core, y], lambda i: kv.at[core, i], kc_send, kc_recv)
    for copy in kc:
        copy.wait()
    kd = exchange(NC, core, lambda i: device(core_=i), lambda i: kv.at[core], lambda i: kv.at[i], kd_send, kd_recv)
    for copy in kd:
        copy.wait()
    for i in range(NC * NY):
        rows = slice(i * 128, (i + 1) * 128)
        kk[rows, :] = kv[i // NY, i % NY, :, 0].reshape(128, D)
        vv[rows, :] = kv[i // NY, i % NY, :, 1].reshape(128, D)
    for i in range(KEYS // KB):
        kt[:, i * KB : (i + 1) * KB] = kk[i * KB : (i + 1) * KB, :].T
    q_copy.wait()
    o_copy.wait()

    def stack(block):
        return jnp.concatenate([block[:, :D], block[:, D:]], axis=0)

    @pl.loop(0, NH)
    def _(t):
        j = rem(t, NH // 2) * 2 + div(t, NH // 2)
        src = partner(j, -1)
        pltpu.make_async_copy(d_vm.at[src], d_vm.at[src], d_recv.at[j]).wait()
        rows = pl.ds(pl.multiple_of(src * T, T), T)
        q = stack(q_vm[rows, :])
        d = stack(d_vm[src])
        o = stack(o_vm[rows, :])
        delta = jnp.sum((d.astype(F32) * o.astype(F32)).T, axis=0, keepdims=True)
        lse = lse_ref[:, rows] * LOG2E
        lse = jnp.concatenate([lse[0:1], lse[1:2]], axis=1)
        dqt = jnp.zeros((D, 2 * T), F32)
        for i in range(KEYS // KB):
            at = slice(i * KB, (i + 1) * KB)
            s = lax.dot_general(kk[at, :], q, NT, preferred_element_type=F32)
            p = jnp.exp2(s * (C * LOG2E) - lse)
            dp = lax.dot_general(vv[at, :], d, NT, preferred_element_type=F32)
            ds = (p * (dp - delta)).astype(BF16)
            acc[1, at, :] += jnp.dot(p.astype(BF16), d, preferred_element_type=F32)
            acc[0, at, :] += jnp.dot(ds, q, preferred_element_type=F32)
            dqt = dqt + jnp.dot(kt[:, at], ds, preferred_element_type=F32)
        dq = (dqt * C).T.astype(BF16)
        dq_vm[rows, 0:D] = dq[0:T]
        dq_vm[rows, D : 2 * D] = dq[T : 2 * T]
        pltpu.make_async_copy(dq_vm.at[rows, :], dq_hbm.at[rows, :], dq_sem.at[j]).start()

    half = KEYS // NC
    part = half // NY
    rd = []
    for i in range(2):
        copy = pltpu.make_async_remote_copy(
            src_ref=acc.at[i, pl.ds(pl.multiple_of((1 - core) * half, half), half)],
            dst_ref=rd_in.at[i], send_sem=rd_send.at[i], recv_sem=rd_recv.at[i],
            device_id=device(core_=1 - core), device_id_type=MESH,
        )
        copy.start()
        rd.append(copy)

    def halves(i, yy):
        mine = pl.ds(pl.multiple_of(core * half + yy * part, part), part)
        return acc[i, mine, :] + rd_in[i, pl.ds(pl.multiple_of(yy * part, part), part), :]

    for i in range(2):
        rd[i].wait()
    for r in range(1, NY):
        to = rem(y + r, NY)
        for i in range(2):
            rc_out[to, i] = halves(i, to).astype(rc_out.dtype)
    rc = exchange(NY, y, lambda i: device(y_=i), lambda i: rc_out.at[i], lambda i: rc_in.at[i], rc_send, rc_recv)
    for i in range(2):
        tot[i] = halves(i, y)
    for r in range(1, NY):
        rc[r - 1].wait()
        tot[...] += rc_in[rem(y + NY - r, NY)].astype(F32)
    for zz in range(NZ):
        rb_out[zz] = tot[:, zz * GROUP : (zz + 1) * GROUP, :].astype(rb_out.dtype)
    rb = exchange(NZ, z, zdev, lambda i: rb_out.at[i], lambda i: rb_in.at[i], rb_send, rb_recv)
    last[...] = tot[:, pl.ds(pl.multiple_of(z * GROUP, GROUP), GROUP), :]
    for r in range(1, NZ):
        rb[r - 1].wait()
        last[...] += rb_in[rem(z + NZ - r, NZ)].astype(F32)
    for p in range(NX):
        ra_out[p, 0:4, :] = last[0, 4 * p : 4 * p + 4, :] * C
        ra_out[p, 4:8, :] = last[1, 4 * p : 4 * p + 4, :]
    ra = exchange(NX, x, lambda i: device(x_=i), lambda i: ra_out.at[i], lambda i: ra_in.at[i], ra_send, ra_recv)
    ra_in[x] = ra_out[x]

    @pl.loop(0, NH)
    def _(j):
        rows = pl.ds(pl.multiple_of(partner(j, -1) * T, T), T)
        pltpu.make_async_copy(dq_vm.at[rows, :], dq_hbm.at[rows, :], dq_sem.at[j]).wait()

    @pl.loop(1, NH)
    def _(j):
        block_copy(j).wait_send()

    for copy in ra:
        copy.wait()
    for g in range(NX):
        dk_ref[:, g * D : (g + 1) * D] = ra_in[g, 0:4, :].astype(BF16)
        dv_ref[:, g * D : (g + 1) * D] = ra_in[g, 4:8, :].astype(BF16)


def on_device(queries, keys, values, outputs, dout, lse):
    tokens = queries.shape[0]
    wire = F32
    dma = pltpu.SemaphoreType.DMA
    part = KEYS // NC // NY
    hbm = pl.BlockSpec(memory_space=pltpu.HBM)
    vmem = pl.BlockSpec(memory_space=pltpu.VMEM)
    flops = 5 * 2 * 2 * tokens * KEYS * D
    return pl.pallas_call(
        kernel,
        out_shape=(
            jax.ShapeDtypeStruct((tokens, 2 * D), BF16),
            jax.ShapeDtypeStruct(keys.shape, BF16),
            jax.ShapeDtypeStruct(values.shape, BF16),
        ),
        in_specs=[hbm, vmem, vmem, hbm, hbm, vmem],
        out_specs=(hbm, vmem, vmem),
        scratch_shapes=[
            pltpu.VMEM((tokens, 2 * D), BF16),
            pltpu.VMEM((tokens, 2 * D), BF16),
            pltpu.VMEM((NH, T, 2 * D), BF16),
            pltpu.VMEM((tokens, 2 * D), BF16),
            pltpu.VMEM((NX, 8, D), F32),
            pltpu.VMEM((NX, 8, D), F32),
            pltpu.VMEM((2, GROUP, D), F32),
            pltpu.VMEM((NC, NY, NZ, 2, GROUP, D), BF16),
            pltpu.VMEM((KEYS, D), BF16),
            pltpu.VMEM((KEYS, D), BF16),
            pltpu.VMEM((D, KEYS), BF16),
            pltpu.VMEM((2, KEYS, D), F32),
            pltpu.VMEM((2, KEYS // NC, D), F32),
            pltpu.VMEM((NY, 2, part, D), wire),
            pltpu.VMEM((NY, 2, part, D), wire),
            pltpu.VMEM((2, part, D), F32),
            pltpu.VMEM((NZ, 2, GROUP, D), wire),
            pltpu.VMEM((NZ, 2, GROUP, D), wire),
            pltpu.VMEM((2, GROUP, D), F32),
            pltpu.VMEM((NX, 8, D), F32),
            pltpu.VMEM((NX, 8, D), F32),
            dma((NH,)), dma((NH,)), dma, dma, dma((NH,)),
            dma((NX,)), dma((NX,)), dma((NZ,)), dma((NZ,)), dma((NY,)), dma((NY,)), dma((NC,)), dma((NC,)),
            dma((2,)), dma((2,)), dma((NY,)), dma((NY,)), dma((NZ,)), dma((NZ,)), dma((NX,)), dma((NX,)),
        ],
        compiler_params=pltpu.CompilerParams(
            collective_id=0, has_side_effects=True, vmem_limit_bytes=56 * 1024 * 1024
        ),
        cost_estimate=pl.CostEstimate(
            flops=flops, bytes_accessed=8 * tokens * 2 * D, transcendentals=2 * tokens * KEYS
        ),
        name="attention_backward",
    )(queries, keys, values, outputs, dout, lse)


def solution(mesh):
    placed = (
        P("ctx", "head"),
        P(("head", "ctx"), None),
        P(("head", "ctx"), None),
        P("ctx", "head"),
        P(("ctx", "head"), None),
        P("head", "ctx"),
    )
    return jax.shard_map(
        on_device,
        mesh=mesh,
        in_specs=placed,
        out_specs=(P("ctx", "head"), P(("head", "ctx"), None), P(("head", "ctx"), None)),
        check_vma=False,
    )
```

time: 1430 us -> 130 us (0.09)
  waiting for transfers between devices: 1210 us -> 0 us
  Pallas kernels: 0 us -> 123 us
  blocking collectives: 83 us -> 0 us
  matrix products: 68.8 us -> 0 us
  local copies, waits for them, and re-layouts: 30.8 us -> 4.24 us
    all_gather x2 -> x0, waiting for transfers between devices: 1040 us -> none  [the longest x1 523 us: on_device(): lax.all_gather(keys, ('head', 'ctx'), axis=0, tiled=True)]
    unnamed x4 -> x0, waiting for transfers between devices: 164 us -> none
    pallas_call x0 -> x1, Pallas kernels: none -> 123 us  [on_device(): pl.pallas_call(kernel, out_shape=(jax.ShapeDtypeStruct((tokens, 2 * D), B...]
    unnamed x1 -> x0, blocking collectives: 83 us -> none
    dot_general x80 -> x0, matrix products: 68.8 us -> none  [the longest x16 32.4 us: on_device(): jnp.dot(q_head, key_group.T, preferred_element_type=jnp.float32) * factor]
    unnamed x67 -> x7, local copies, waits for them, and re-layouts: 23.2 us -> 4.24 us
  transfers between devices with their start and end apart: 4 -> 0, of which waited for: 3 -> 0; matrix products, arithmetic and copies ran while one was open for 4% -> 0% of each run, Pallas kernels for 0% -> 0%
where the time goes in v1:
time: 130 us; the launch traced here: 128 us
  Pallas kernels  123 us (95%)
  local copies, waits for them, and re-layouts  4.24 us (3%)
    pallas_call x1, Pallas kernels, on_device(): pl.pallas_call(kernel, out_shape=(jax.ShapeDtypeStruct((tokens, 2 * D), B...  123 us
    unnamed x7, local copies, waits for them, and re-layouts  4.24 us

profile of v1, /device:TPU:32, one launch (start us, length us, event | category | flops | bytes accessed | tf_op | source)
XLA Modules:
  0.0 128.1 jit_solution(10623403662397797324)
XLA Ops:
  0.6 123.2 %attention_backward.1 = (bf16[4096,256]{1,0:T(8,128)(2,1)}, bf16[4,512]{1,0:T(4,128)(2,1)}, bf16[4,512]{1,0:T(4,128)(2,1)}) custom-call(bf16[4096,256]{1,0:T(8,128)(2,1)} %q_hbm.1, bf16[4,512]{1,0:T(4,128)(2,1)} %k_ref.1, bf16[4,512]{1,0:T(4,128)(2,1)} %v_ref.1, bf16[4096,256]{1,0:T(8,128)(2,1)} %o_hbm.1, bf16[128,8192]{1,0:T(8,128)(2,1)} %d_hbm.1, ...), custom_call_target="tpu_custom_call" | custom-call | flops 10737418240 | bytes 8388608 | tf_op jit(solution)/shard_map/attention_backward/pallas_call | solution.py:237
  123.9 0.0 copy-start.1
  123.9 0.0 copy-start
  123.9 3.0 %copy.12 = bf16[4096,256]{1,0:T(8,128)(2,1)} copy(bf16[4096,256]{1,0:T(8,128)(2,1)} %get-tuple-element.6) | data formatting | bytes 4194304
  126.9 0.0 copy-done.1
  126.9 0.6 copy.13
  127.5 0.0 copy-done
  127.5 0.6 copy.14
Async XLA Ops:
  123.9 3.1 %copy-start.1 = (bf16[4,512]{1,0:T(4,128)(2,1)S(1)}, bf16[4,512]{1,0:T(4,128)(2,1)}, u32[]{:S(2)}) copy-start(bf16[4,512]{1,0:T(4,128)(2,1)} %get-tuple-element.7) | copy-start | bytes 12292
  123.9 3.7 %copy-start = (bf16[4,512]{1,0:T(4,128)(2,1)S(1)}, bf16[4,512]{1,0:T(4,128)(2,1)}, u32[]{:S(2)}) copy-start(bf16[4,512]{1,0:T(4,128)(2,1)} %get-tuple-element.8) | copy-start | bytes 12292

commit v2 on v1

--- a/solution.py
+++ b/solution.py
@@ -17,6 +17,8 @@
 KEYS = 1024
 GROUP = 16
 KB = 256
+PACE = (6, 6, 8)
+FINISH = 8
 C = D ** (-0.5)
 LOG2E = math.log2(math.e)
 NT = (((1,), (1,)), ((), ()))
@@ -33,11 +35,11 @@
 
 def kernel(
     q_hbm, k_ref, v_ref, o_hbm, d_hbm, lse_ref,
-    dq_hbm, dk_ref, dv_ref,
-    q_vm, o_vm, d_vm, dq_vm,
+    dq_vm, ra_in,
+    q_vm, o_vm, d_vm,
     a_out, a_in, kv16, kv, kk, vv, kt,
-    acc, rd_in, rc_out, rc_in, tot, rb_out, rb_in, last, ra_out, ra_in,
-    d_send, d_recv, q_sem, o_sem, dq_sem,
+    acc, rd_in, rc_out, rc_in, tot, rb_out, rb_in, last, ra_out,
+    d_send, d_recv, q_sem, o_sem,
     ka_send, ka_recv, kb_send, kb_recv, kc_send, kc_recv, kd_send, kd_recv,
     rd_send, rd_recv, rc_send, rc_recv, rb_send, rb_recv, ra_send, ra_recv,
 ):
@@ -51,10 +53,12 @@
         return ((x_ * NZL + zl_) * NC + core_, y_ * NZH + zh_)
 
     def partner(j, way):
-        da, dc, db, dx = rem(j, 2), rem(div(j, 2), 2), rem(div(j, 4), 2), div(j, 8)
-        x_ = rem(x + NX + way * dx, NX)
+        da, dx, dc, db = rem(j, 2), rem(div(j, 2), NX), rem(div(j, 2 * NX), 2), div(j, 4 * NX)
+        core_ = rem(core + dc, NC)
+        turn = way * (1 - 2 * (core if way == 1 else core_))
+        x_ = rem(x + NX + turn * dx, NX)
         zl_ = rem(za + da, 2) * 2 + rem(zb + db, 2)
-        return (x_ * NZL + zl_) * NC + rem(core + dc, NC)
+        return (x_ * NZL + zl_) * NC + core_
 
     q_copy = pltpu.make_async_copy(q_hbm, q_vm, q_sem)
     o_copy = pltpu.make_async_copy(o_hbm, o_vm, o_sem)
@@ -74,9 +78,6 @@
         pl.semaphore_signal(
             barrier, inc=1, device_id=device(zl_=rem(zl + r, NZL), zh_=1 - zh), device_id_type=MESH
         )
-    own.start()
-    q_copy.start()
-    o_copy.start()
     for g in range(NX):
         a_out[g, 0:4, :] = k_ref[:, g * D : (g + 1) * D].astype(F32)
         a_out[g, 4:8, :] = v_ref[:, g * D : (g + 1) * D].astype(F32)
@@ -105,10 +106,12 @@
             device_id=(to, ctx), device_id_type=MESH,
         )
 
-    @pl.loop(1, NH)
-    def _(j):
-        block_copy(j).start()
-
+    def start_blocks(first, end):
+        @pl.loop(first, end)
+        def _(j):
+            block_copy(j).start()
+
+    start_blocks(1, 1 + PACE[0])
     a_in[x] = a_out[x]
     for copy in ka:
         copy.wait()
@@ -121,15 +124,29 @@
         return device(zl_=rem(i, NZL), zh_=div(i, NZL))
 
     kb = exchange(NZ, z, zdev, lambda i: kv.at[core, y, z], lambda i: kv.at[core, y, i], kb_send, kb_recv)
+    start_blocks(1 + PACE[0], 1 + PACE[0] + PACE[1])
+    own.start()
+    q_copy.start()
+    o_copy.start()
     acc[...] = jnp.zeros_like(acc)
     for copy in kb:
         copy.wait()
     kc = exchange(NY, y, lambda i: device(y_=i), lambda i: kv.at[core, y], lambda i: kv.at[core, i], kc_send, kc_recv)
-    for copy in kc:
-        copy.wait()
-    kd = exchange(NC, core, lambda i: device(core_=i), lambda i: kv.at[core], lambda i: kv.at[i], kd_send, kd_recv)
-    for copy in kd:
-        copy.wait()
+
+    def sibling(r):
+        at = rem(y + NY - r, NY)
+        return pltpu.make_async_remote_copy(
+            src_ref=kv.at[core, at], dst_ref=kv.at[core, at], send_sem=kd_send.at[r], recv_sem=kd_recv.at[r],
+            device_id=device(core_=1 - core), device_id_type=MESH,
+        )
+
+    sibling(0).start()
+    start_blocks(1 + PACE[0] + PACE[1], 1 + sum(PACE))
+    for r in range(1, NY):
+        kc[r - 1].wait()
+        sibling(r).start()
+    for r in range(NY):
+        sibling(r).wait()
     for i in range(NC * NY):
         rows = slice(i * 128, (i + 1) * 128)
         kk[rows, :] = kv[i // NY, i % NY, :, 0].reshape(128, D)
@@ -142,19 +159,29 @@
     def stack(block):
         return jnp.concatenate([block[:, :D], block[:, D:]], axis=0)
 
-    @pl.loop(0, NH)
-    def _(t):
-        j = rem(t, NH // 2) * 2 + div(t, NH // 2)
+    def arrived(j):
         src = partner(j, -1)
         pltpu.make_async_copy(d_vm.at[src], d_vm.at[src], d_recv.at[j]).wait()
-        rows = pl.ds(pl.multiple_of(src * T, T), T)
-        q = stack(q_vm[rows, :])
-        d = stack(d_vm[src])
-        o = stack(o_vm[rows, :])
+        return src
+
+    @pl.loop(0, NH, step=2)
+    def _(j):
+        for i in range(2):
+            ahead = 1 + sum(PACE) + j + i
+
+            @pl.when(ahead < NH)
+            def _():
+                block_copy(ahead).start()
+
+        pair = [arrived(j), arrived(j + 1)]
+        rows = [pl.ds(pl.multiple_of(src * T, T), T) for src in pair]
+        q = jnp.concatenate([stack(q_vm[at, :]) for at in rows], axis=0)
+        d = jnp.concatenate([stack(d_vm[src]) for src in pair], axis=0)
+        o = jnp.concatenate([stack(o_vm[at, :]) for at in rows], axis=0)
         delta = jnp.sum((d.astype(F32) * o.astype(F32)).T, axis=0, keepdims=True)
-        lse = lse_ref[:, rows] * LOG2E
-        lse = jnp.concatenate([lse[0:1], lse[1:2]], axis=1)
-        dqt = jnp.zeros((D, 2 * T), F32)
+        lse = [lse_ref[:, at] * LOG2E for at in rows]
+        lse = jnp.concatenate([row for pairs in lse for row in (pairs[0:1], pairs[1:2])], axis=1)
+        dqt = jnp.zeros((D, 4 * T), F32)
         for i in range(KEYS // KB):
             at = slice(i * KB, (i + 1) * KB)
             s = lax.dot_general(kk[at, :], q, NT, preferred_element_type=F32)
@@ -165,44 +192,48 @@
             acc[0, at, :] += jnp.dot(ds, q, preferred_element_type=F32)
             dqt = dqt + jnp.dot(kt[:, at], ds, preferred_element_type=F32)
         dq = (dqt * C).T.astype(BF16)
-        dq_vm[rows, 0:D] = dq[0:T]
-        dq_vm[rows, D : 2 * D] = dq[T : 2 * T]
-        pltpu.make_async_copy(dq_vm.at[rows, :], dq_hbm.at[rows, :], dq_sem.at[j]).start()
+        for i in range(2):
+            dq_vm[rows[i], 0:D] = dq[2 * i * T : (2 * i + 1) * T]
+            dq_vm[rows[i], D : 2 * D] = dq[(2 * i + 1) * T : (2 * i + 2) * T]
 
     half = KEYS // NC
     part = half // NY
     rd = []
-    for i in range(2):
+    for r in (1, 2, 3, 0):
+        to = rem(y + r, NY)
         copy = pltpu.make_async_remote_copy(
-            src_ref=acc.at[i, pl.ds(pl.multiple_of((1 - core) * half, half), half)],
-            dst_ref=rd_in.at[i], send_sem=rd_send.at[i], recv_sem=rd_recv.at[i],
+            src_ref=acc.at[:, pl.ds(pl.multiple_of((1 - core) * half + to * part, part), part), :],
+            dst_ref=rd_in.at[to], send_sem=rd_send.at[r], recv_sem=rd_recv.at[r],
             device_id=device(core_=1 - core), device_id_type=MESH,
         )
         copy.start()
         rd.append(copy)
 
-    def halves(i, yy):
-        mine = pl.ds(pl.multiple_of(core * half + yy * part, part), part)
-        return acc[i, mine, :] + rd_in[i, pl.ds(pl.multiple_of(yy * part, part), part), :]
-
-    for i in range(2):
-        rd[i].wait()
+    def both(yy):
+        return acc[:, pl.ds(pl.multiple_of(core * half + yy * part, part), part), :] + rd_in[yy]
+
+    rc = []
     for r in range(1, NY):
         to = rem(y + r, NY)
-        for i in range(2):
-            rc_out[to, i] = halves(i, to).astype(rc_out.dtype)
-    rc = exchange(NY, y, lambda i: device(y_=i), lambda i: rc_out.at[i], lambda i: rc_in.at[i], rc_send, rc_recv)
-    for i in range(2):
-        tot[i] = halves(i, y)
+        rd[r - 1].wait_recv()
+        rc_out[to] = both(to).astype(rc_out.dtype)
+        copy = pltpu.make_async_remote_copy(
+            src_ref=rc_out.at[to], dst_ref=rc_in.at[y], send_sem=rc_send.at[r], recv_sem=rc_recv.at[r],
+            device_id=device(y_=to), device_id_type=MESH,
+        )
+        copy.start()
+        rc.append(copy)
+    rd[NY - 1].wait_recv()
+    tot[...] = both(y)
     for r in range(1, NY):
-        rc[r - 1].wait()
+        rc[r - 1].wait_recv()
         tot[...] += rc_in[rem(y + NY - r, NY)].astype(F32)
     for zz in range(NZ):
         rb_out[zz] = tot[:, zz * GROUP : (zz + 1) * GROUP, :].astype(rb_out.dtype)
     rb = exchange(NZ, z, zdev, lambda i: rb_out.at[i], lambda i: rb_in.at[i], rb_send, rb_recv)
     last[...] = tot[:, pl.ds(pl.multiple_of(z * GROUP, GROUP), GROUP), :]
     for r in range(1, NZ):
-        rb[r - 1].wait()
+        rb[r - 1].wait_recv()
         last[...] += rb_in[rem(z + NZ - r, NZ)].astype(F32)
     for p in range(NX):
         ra_out[p, 0:4, :] = last[0, 4 * p : 4 * p + 4, :] * C
@@ -210,44 +241,51 @@
     ra = exchange(NX, x, lambda i: device(x_=i), lambda i: ra_out.at[i], lambda i: ra_in.at[i], ra_send, ra_recv)
     ra_in[x] = ra_out[x]
 
-    @pl.loop(0, NH)
-    def _(j):
-        rows = pl.ds(pl.multiple_of(partner(j, -1) * T, T), T)
-        pltpu.make_async_copy(dq_vm.at[rows, :], dq_hbm.at[rows, :], dq_sem.at[j]).wait()
-
     @pl.loop(1, NH)
     def _(j):
         block_copy(j).wait_send()
 
+    for copy in rd + rc + rb:
+        copy.wait_send()
     for copy in ra:
         copy.wait()
+
+
+def finish(dq_in, terms, dq_hbm, dk_ref, dv_ref, sem):
+    rows = dq_in.shape[0] // FINISH
+    copies = [
+        pltpu.make_async_copy(dq_in.at[i * rows : (i + 1) * rows], dq_hbm.at[i * rows : (i + 1) * rows], sem.at[i])
+        for i in range(FINISH)
+    ]
+    for copy in copies:
+        copy.start()
     for g in range(NX):
-        dk_ref[:, g * D : (g + 1) * D] = ra_in[g, 0:4, :].astype(BF16)
-        dv_ref[:, g * D : (g + 1) * D] = ra_in[g, 4:8, :].astype(BF16)
+        dk_ref[:, g * D : (g + 1) * D] = terms[g, 0:4, :].astype(BF16)
+        dv_ref[:, g * D : (g + 1) * D] = terms[g, 4:8, :].astype(BF16)
+    for copy in copies:
+        copy.wait()
 
 
 def on_device(queries, keys, values, outputs, dout, lse):
     tokens = queries.shape[0]
-    wire = F32
+    wire = BF16
     dma = pltpu.SemaphoreType.DMA
     part = KEYS // NC // NY
     hbm = pl.BlockSpec(memory_space=pltpu.HBM)
     vmem = pl.BlockSpec(memory_space=pltpu.VMEM)
     flops = 5 * 2 * 2 * tokens * KEYS * D
-    return pl.pallas_call(
+    dq, terms = pl.pallas_call(
         kernel,
         out_shape=(
-            jax.ShapeDtypeStruct((tokens, 2 * D), BF16),
-            jax.ShapeDtypeStruct(keys.shape, BF16),
-            jax.ShapeDtypeStruct(values.shape, BF16),
+            pltpu.VMEM((tokens, 2 * D), BF16),
+            jax.ShapeDtypeStruct((NX, 8, D), F32),
         ),
         in_specs=[hbm, vmem, vmem, hbm, hbm, vmem],
-        out_specs=(hbm, vmem, vmem),
+        out_specs=(vmem, vmem),
         scratch_shapes=[
             pltpu.VMEM((tokens, 2 * D), BF16),
             pltpu.VMEM((tokens, 2 * D), BF16),
             pltpu.VMEM((NH, T, 2 * D), BF16),
-            pltpu.VMEM((tokens, 2 * D), BF16),
             pltpu.VMEM((NX, 8, D), F32),
             pltpu.VMEM((NX, 8, D), F32),
             pltpu.VMEM((2, GROUP, D), F32),
@@ -256,7 +294,7 @@
             pltpu.VMEM((KEYS, D), BF16),
             pltpu.VMEM((D, KEYS), BF16),
             pltpu.VMEM((2, KEYS, D), F32),
-            pltpu.VMEM((2, KEYS // NC, D), F32),
+            pltpu.VMEM((NY, 2, part, D), F32),
             pltpu.VMEM((NY, 2, part, D), wire),
             pltpu.VMEM((NY, 2, part, D), wire),
             pltpu.VMEM((2, part, D), F32),
@@ -264,10 +302,9 @@
             pltpu.VMEM((NZ, 2, GROUP, D), wire),
             pltpu.VMEM((2, GROUP, D), F32),
             pltpu.VMEM((NX, 8, D), F32),
-            pltpu.VMEM((NX, 8, D), F32),
-            dma((NH,)), dma((NH,)), dma, dma, dma((NH,)),
-            dma((NX,)), dma((NX,)), dma((NZ,)), dma((NZ,)), dma((NY,)), dma((NY,)), dma((NC,)), dma((NC,)),
-            dma((2,)), dma((2,)), dma((NY,)), dma((NY,)), dma((NZ,)), dma((NZ,)), dma((NX,)), dma((NX,)),
+            dma((NH,)), dma((NH,)), dma, dma,
+            dma((NX,)), dma((NX,)), dma((NZ,)), dma((NZ,)), dma((NY,)), dma((NY,)), dma((NY,)), dma((NY,)),
+            dma((NY,)), dma((NY,)), dma((NY,)), dma((NY,)), dma((NZ,)), dma((NZ,)), dma((NX,)), dma((NX,)),
         ],
         compiler_params=pltpu.CompilerParams(
             collective_id=0, has_side_effects=True, vmem_limit_bytes=56 * 1024 * 1024
@@ -277,6 +314,20 @@
         ),
         name="attention_backward",
     )(queries, keys, values, outputs, dout, lse)
+    dq = pltpu.with_memory_space_constraint(dq, pltpu.VMEM)
+    return pl.pallas_call(
+        finish,
+        out_shape=(
+            jax.ShapeDtypeStruct(dq.shape, BF16),
+            jax.ShapeDtypeStruct(keys.shape, BF16),
+            jax.ShapeDtypeStruct(values.shape, BF16),
+        ),
+        in_specs=[vmem, vmem],
+        out_specs=(hbm, vmem, vmem),
+        scratch_shapes=[dma((FINISH,))],
+        cost_estimate=pl.CostEstimate(flops=0, bytes_accessed=4 * tokens * 2 * D, transcendentals=0),
+        name="finish",
+    )(dq, terms)
 
 
 def solution(mesh):

time: 130 us -> 81.1 us (0.62); the launches traced: 128 us -> 80.9 us
  Pallas kernels: 123 us -> 80.3 us
  local copies, waits for them, and re-layouts: 4.24 us -> 0 us
    pallas_call x1 -> x2, Pallas kernels: 123 us -> 80.3 us  [the longest x1 77.6 us: on_device(): pl.pallas_call(kernel, out_shape=(pltpu.VMEM((tokens, 2 * D), BF16), jax....]
    unnamed x7 -> x0, local copies, waits for them, and re-layouts: 4.24 us -> none
where the time goes in v2:
time: 81.1 us; the launch traced here: 80.9 us
  Pallas kernels  80.3 us (99%)
    pallas_call x1, Pallas kernels, on_device(): pl.pallas_call(kernel, out_shape=(pltpu.VMEM((tokens, 2 * D), BF16), jax....  77.6 us
    pallas_call x1, Pallas kernels, on_device(): pl.pallas_call(finish, out_shape=(jax.ShapeDtypeStruct(dq.shape, BF16), j...  2.69 us

profile of v2, /device:TPU:32, one launch (start us, length us, event | category | flops | bytes accessed | tf_op | source)
XLA Modules:
  0.0 80.9 jit_solution(2104006638549630077)
XLA Ops:
  0.6 77.6 %attention_backward.1 = (bf16[4096,256]{1,0:T(8,128)(2,1)S(1)}, f32[4,8,128]{2,1,0:T(8,128)}) custom-call(bf16[4096,256]{1,0:T(8,128)(2,1)} %q_hbm.1, bf16[4,512]{1,0:T(4,128)(2,1)} %k_ref.1, bf16[4,512]{1,0:T(4,128)(2,1)} %v_ref.1, bf16[4096,256]{1,0:T(8,128)(2,1)} %o_hbm.1, bf16[128,8192]{1,0:T(8,128)(2,1)} %d_hbm.1, f32[2,4096]{1,0:T(2,128)} %lse_ref.1), custom_call_target="tpu_custom_call" | custom-call | flops 10737418240 | bytes 8388608 | tf_op jit(solution)/shard_map/attention_backward/pallas_call | solution.py:277
  78.3 2.7 %finish.1 = (bf16[4096,256]{1,0:T(8,128)(2,1)}, bf16[4,512]{1,0:T(4,128)(2,1)}, bf16[4,512]{1,0:T(4,128)(2,1)}) custom-call(bf16[4096,256]{1,0:T(8,128)(2,1)S(1)} %get-tuple-element.5.dq_in, f32[4,8,128]{2,1,0:T(8,128)} %get-tuple-element.6.terms), custom_call_target="tpu_custom_call" | custom-call | bytes 4194304 | tf_op jit(solution)/shard_map/finish/pallas_call | solution.py:318

commit v3 on v2

--- a/solution.py
+++ b/solution.py
@@ -17,8 +17,9 @@
 KEYS = 1024
 GROUP = 16
 KB = 256
+AHEAD = 12
 PACE = (6, 6, 8)
-FINISH = 8
+FINISH = 4
 C = D ** (-0.5)
 LOG2E = math.log2(math.e)
 NT = (((1,), (1,)), ((), ()))
@@ -85,7 +86,7 @@
 
     def exchange(n, me, target, src, dst, send, recv):
         copies = []
-        for r in range(1, n):
+        for r in sorted(range(1, n), key=lambda r: -min(r, n - r)):
             to = rem(me + r, n)
             copy = pltpu.make_async_remote_copy(
                 src_ref=src(to), dst_ref=dst(me), send_sem=send.at[r], recv_sem=recv.at[r],
@@ -142,8 +143,8 @@
 
     sibling(0).start()
     start_blocks(1 + PACE[0] + PACE[1], 1 + sum(PACE))
-    for r in range(1, NY):
-        kc[r - 1].wait()
+    for i, r in enumerate((2, 1, 3)):
+        kc[i].wait()
         sibling(r).start()
     for r in range(NY):
         sibling(r).wait()
@@ -167,9 +168,9 @@
     @pl.loop(0, NH, step=2)
     def _(j):
         for i in range(2):
-            ahead = 1 + sum(PACE) + j + i
-
-            @pl.when(ahead < NH)
+            ahead = AHEAD + j + i
+
+            @pl.when((ahead > sum(PACE)) & (ahead < NH))
             def _():
                 block_copy(ahead).start()
 
@@ -199,7 +200,7 @@
     half = KEYS // NC
     part = half // NY
     rd = []
-    for r in (1, 2, 3, 0):
+    for r in (2, 1, 3, 0):
         to = rem(y + r, NY)
         copy = pltpu.make_async_remote_copy(
             src_ref=acc.at[:, pl.ds(pl.multiple_of((1 - core) * half + to * part, part), part), :],
@@ -213,9 +214,9 @@
         return acc[:, pl.ds(pl.multiple_of(core * half + yy * part, part), part), :] + rd_in[yy]
 
     rc = []
-    for r in range(1, NY):
+    for i, r in enumerate((2, 1, 3)):
         to = rem(y + r, NY)
-        rd[r - 1].wait_recv()
+        rd[i].wait_recv()
         rc_out[to] = both(to).astype(rc_out.dtype)
         copy = pltpu.make_async_remote_copy(
             src_ref=rc_out.at[to], dst_ref=rc_in.at[y], send_sem=rc_send.at[r], recv_sem=rc_recv.at[r],
@@ -225,16 +226,19 @@
         rc.append(copy)
     rd[NY - 1].wait_recv()
     tot[...] = both(y)
-    for r in range(1, NY):
-        rc[r - 1].wait_recv()
+    for i, r in enumerate((2, 1, 3)):
+        rc[i].wait_recv()
         tot[...] += rc_in[rem(y + NY - r, NY)].astype(F32)
     for zz in range(NZ):
         rb_out[zz] = tot[:, zz * GROUP : (zz + 1) * GROUP, :].astype(rb_out.dtype)
     rb = exchange(NZ, z, zdev, lambda i: rb_out.at[i], lambda i: rb_in.at[i], rb_send, rb_recv)
     last[...] = tot[:, pl.ds(pl.multiple_of(z * GROUP, GROUP), GROUP), :]
+    for copy in rb:
+        copy.wait_recv()
+    terms = last[...]
     for r in range(1, NZ):
-        rb[r - 1].wait_recv()
-        last[...] += rb_in[rem(z + NZ - r, NZ)].astype(F32)
+        terms = terms + rb_in[rem(z + NZ - r, NZ)].astype(F32)
+    last[...] = terms
     for p in range(NX):
         ra_out[p, 0:4, :] = last[0, 4 * p : 4 * p + 4, :] * C
         ra_out[p, 4:8, :] = last[1, 4 * p : 4 * p + 4, :]
@@ -251,7 +255,7 @@
         copy.wait()
 
 
-def finish(dq_in, terms, dq_hbm, dk_ref, dv_ref, sem):
+def finish(dq_in, terms, dq_hbm, dk_hbm, dv_hbm, low, sem):
     rows = dq_in.shape[0] // FINISH
     copies = [
         pltpu.make_async_copy(dq_in.at[i * rows : (i + 1) * rows], dq_hbm.at[i * rows : (i + 1) * rows], sem.at[i])
@@ -259,9 +263,12 @@
     ]
     for copy in copies:
         copy.start()
-    for g in range(NX):
-        dk_ref[:, g * D : (g + 1) * D] = terms[g, 0:4, :].astype(BF16)
-        dv_ref[:, g * D : (g + 1) * D] = terms[g, 4:8, :].astype(BF16)
+    for i, out in enumerate((dk_hbm, dv_hbm)):
+        for g in range(NX):
+            low[i, :, g * D : (g + 1) * D] = terms[g, 4 * i : 4 * i + 4, :].astype(BF16)
+        copy = pltpu.make_async_copy(low.at[i], out, sem.at[FINISH + i])
+        copy.start()
+        copies.append(copy)
     for copy in copies:
         copy.wait()
 
@@ -278,7 +285,7 @@
         kernel,
         out_shape=(
             pltpu.VMEM((tokens, 2 * D), BF16),
-            jax.ShapeDtypeStruct((NX, 8, D), F32),
+            pltpu.VMEM((NX, 8, D), F32),
         ),
         in_specs=[hbm, vmem, vmem, hbm, hbm, vmem],
         out_specs=(vmem, vmem),
@@ -314,7 +321,7 @@
         ),
         name="attention_backward",
     )(queries, keys, values, outputs, dout, lse)
-    dq = pltpu.with_memory_space_constraint(dq, pltpu.VMEM)
+    dq, terms = (pltpu.with_memory_space_constraint(a, pltpu.VMEM) for a in (dq, terms))
     return pl.pallas_call(
         finish,
         out_shape=(
@@ -323,8 +330,8 @@
             jax.ShapeDtypeStruct(values.shape, BF16),
         ),
         in_specs=[vmem, vmem],
-        out_specs=(hbm, vmem, vmem),
-        scratch_shapes=[dma((FINISH,))],
+        out_specs=(hbm, hbm, hbm),
+        scratch_shapes=[pltpu.VMEM((2, *keys.shape), BF16), dma((FINISH + 2,))],
         cost_estimate=pl.CostEstimate(flops=0, bytes_accessed=4 * tokens * 2 * D, transcendentals=0),
         name="finish",
     )(dq, terms)

time: 81.1 us -> 78.5 us (0.968)
  Pallas kernels: 80.3 us -> 77.7 us
    pallas_call x1, Pallas kernels: 2.69 us -> 1.37 us  [on_device(): pl.pallas_call(finish, out_shape=(jax.ShapeDtypeStruct(dq.shape, BF16), j...]
    pallas_call x1, Pallas kernels: 77.6 us -> 76.4 us  [on_device(): pl.pallas_call(kernel, out_shape=(pltpu.VMEM((tokens, 2 * D), BF16), pltp...]
where the time goes in v3:
time: 78.5 us; the launch traced here: 78.4 us
  Pallas kernels  77.7 us (99%)
    pallas_call x1, Pallas kernels, on_device(): pl.pallas_call(kernel, out_shape=(pltpu.VMEM((tokens, 2 * D), BF16), pltp...  76.4 us

profile of v3, /device:TPU:32, one launch (start us, length us, event | category | flops | bytes accessed | tf_op | source)
XLA Modules:
  0.0 78.4 jit_solution(1993648263868162117)
XLA Ops:
  0.6 76.4 %attention_backward.1 = (bf16[4096,256]{1,0:T(8,128)(2,1)S(1)}, f32[4,8,128]{2,1,0:T(8,128)S(1)}) custom-call(bf16[4096,256]{1,0:T(8,128)(2,1)} %q_hbm.1, bf16[4,512]{1,0:T(4,128)(2,1)} %k_ref.1, bf16[4,512]{1,0:T(4,128)(2,1)} %v_ref.1, bf16[4096,256]{1,0:T(8,128)(2,1)} %o_hbm.1, bf16[128,8192]{1,0:T(8,128)(2,1)} %d_hbm.1, f32[2,4096]{1,0:T(2,128)} %lse_ref.1), custom_call_target="tpu_custom_call" | custom-call | flops 10737418240 | bytes 8388608 | tf_op jit(solution)/shard_map/attention_backward/pallas_call | solution.py:284
  77.0 1.4 %finish.1 = (bf16[4096,256]{1,0:T(8,128)(2,1)}, bf16[4,512]{1,0:T(4,128)(2,1)}, bf16[4,512]{1,0:T(4,128)(2,1)}) custom-call(bf16[4096,256]{1,0:T(8,128)(2,1)S(1)} %get-tuple-element.5.dq_in, f32[4,8,128]{2,1,0:T(8,128)S(1)} %get-tuple-element.6.terms), custom_call_target="tpu_custom_call" | custom-call | bytes 4194304 | tf_op jit(solution)/shard_map/finish/pallas_call | solution.py:325

commit v4 on v3

--- a/solution.py
+++ b/solution.py
@@ -165,15 +165,19 @@
         pltpu.make_async_copy(d_vm.at[src], d_vm.at[src], d_recv.at[j]).wait()
         return src
 
-    @pl.loop(0, NH, step=2)
-    def _(j):
-        for i in range(2):
-            ahead = AHEAD + j + i
-
-            @pl.when((ahead > sum(PACE)) & (ahead < NH))
-            def _():
-                block_copy(ahead).start()
-
+    half = KEYS // NC
+    part = half // NY
+    rd = []
+    for r in (2, 1, 3, 0):
+        to = rem(y + r, NY)
+        copy = pltpu.make_async_remote_copy(
+            src_ref=acc.at[:, pl.ds(pl.multiple_of((1 - core) * half + to * part, part), part), :],
+            dst_ref=rd_in.at[to], send_sem=rd_send.at[r], recv_sem=rd_recv.at[r],
+            device_id=device(core_=1 - core), device_id_type=MESH,
+        )
+        rd.append(copy)
+
+    def compute(j, last_pair):
         pair = [arrived(j), arrived(j + 1)]
         rows = [pl.ds(pl.multiple_of(src * T, T), T) for src in pair]
         q = jnp.concatenate([stack(q_vm[at, :]) for at in rows], axis=0)
@@ -184,7 +188,10 @@
         lse = jnp.concatenate([row for pairs in lse for row in (pairs[0:1], pairs[1:2])], axis=1)
         dqt = jnp.zeros((D, 4 * T), F32)
         for i in range(KEYS // KB):
-            at = slice(i * KB, (i + 1) * KB)
+            at = pl.ds(i * KB, KB)
+            if last_pair:
+                turn = rem((1 - core) * (half // KB) + i, KEYS // KB)
+                at = pl.ds(pl.multiple_of(turn * KB, KB), KB)
             s = lax.dot_general(kk[at, :], q, NT, preferred_element_type=F32)
             p = jnp.exp2(s * (C * LOG2E) - lse)
             dp = lax.dot_general(vv[at, :], d, NT, preferred_element_type=F32)
@@ -192,23 +199,26 @@
             acc[1, at, :] += jnp.dot(p.astype(BF16), d, preferred_element_type=F32)
             acc[0, at, :] += jnp.dot(ds, q, preferred_element_type=F32)
             dqt = dqt + jnp.dot(kt[:, at], ds, preferred_element_type=F32)
+            if last_pair and (i + 1) * KB == half:
+                for copy in rd:
+                    copy.start()
         dq = (dqt * C).T.astype(BF16)
         for i in range(2):
             dq_vm[rows[i], 0:D] = dq[2 * i * T : (2 * i + 1) * T]
             dq_vm[rows[i], D : 2 * D] = dq[(2 * i + 1) * T : (2 * i + 2) * T]
 
-    half = KEYS // NC
-    part = half // NY
-    rd = []
-    for r in (2, 1, 3, 0):
-        to = rem(y + r, NY)
-        copy = pltpu.make_async_remote_copy(
-            src_ref=acc.at[:, pl.ds(pl.multiple_of((1 - core) * half + to * part, part), part), :],
-            dst_ref=rd_in.at[to], send_sem=rd_send.at[r], recv_sem=rd_recv.at[r],
-            device_id=device(core_=1 - core), device_id_type=MESH,
-        )
-        copy.start()
-        rd.append(copy)
+    @pl.loop(0, NH - 2, step=2)
+    def _(j):
+        for i in range(2):
+            ahead = AHEAD + j + i
+
+            @pl.when((ahead > sum(PACE)) & (ahead < NH))
+            def _():
+                block_copy(ahead).start()
+
+        compute(j, False)
+
+    compute(jnp.int32(NH - 2), True)
 
     def both(yy):
         return acc[:, pl.ds(pl.multiple_of(core * half + yy * part, part), part), :] + rd_in[yy]

time: 78.5 us -> 78.2 us (level)
  no operation moved by 1% of the time
where the time goes in v4:
time: 78.2 us; the launch traced here: 78 us
  Pallas kernels  77.4 us (99%)
    pallas_call x1, Pallas kernels, on_device(): pl.pallas_call(kernel, out_shape=(pltpu.VMEM((tokens, 2 * D), BF16), pltp...  76 us

profile of v4, /device:TPU:32, one launch (start us, length us, event | category | flops | bytes accessed | tf_op | source)
XLA Modules:
  0.0 78.0 jit_solution(18163434100433277352)
XLA Ops:
  0.6 76.0 %attention_backward.1 = (bf16[4096,256]{1,0:T(8,128)(2,1)S(1)}, f32[4,8,128]{2,1,0:T(8,128)S(1)}) custom-call(bf16[4096,256]{1,0:T(8,128)(2,1)} %q_hbm.1, bf16[4,512]{1,0:T(4,128)(2,1)} %k_ref.1, bf16[4,512]{1,0:T(4,128)(2,1)} %v_ref.1, bf16[4096,256]{1,0:T(8,128)(2,1)} %o_hbm.1, bf16[128,8192]{1,0:T(8,128)(2,1)} %d_hbm.1, f32[2,4096]{1,0:T(2,128)} %lse_ref.1), custom_call_target="tpu_custom_call" | custom-call | flops 10737418240 | bytes 8388608 | tf_op jit(solution)/shard_map/attention_backward/pallas_call | solution.py:294
  76.6 1.4 %finish.1 = (bf16[4096,256]{1,0:T(8,128)(2,1)}, bf16[4,512]{1,0:T(4,128)(2,1)}, bf16[4,512]{1,0:T(4,128)(2,1)}) custom-call(bf16[4096,256]{1,0:T(8,128)(2,1)S(1)} %get-tuple-element.5.dq_in, f32[4,8,128]{2,1,0:T(8,128)S(1)} %get-tuple-element.6.terms), custom_call_target="tpu_custom_call" | custom-call | bytes 4194304 | tf_op jit(solution)/shard_map/finish/pallas_call | solution.py:335
